TPU v7x, 256 devices: a whole 4x4x8 slice. The times are simulated.
256 devices in a mesh: band: 8 (over x, y_lo), grid: 32 (over y_hi, z, core).
Axes of the slice: x: 4, y: 4 (y_hi: 2, y_lo: 2; y = y_hi * 2 + y_lo), z: 8, core: 2. Of those that a mesh axis runs over, the one named last changes fastest.
Arguments:
- orbitals: float32 [16, 128, 128, 128], P('band', 'grid'), may hold values from -3 to 3
Outputs:
- exchange_terms: float32 [16, 128, 128, 128], P('band', 'grid')
All inputs are finite; a program needn't handle non-finite values.
Results may differ from a plain program's by a relative error of at most 0.0003.
Values sent between devices are 32-bit elements; how exact they have to be, the bound alone decides.
A program may use at most 64 MiB of HBM per device.

v0:
```python
import functools
import math

import jax
import jax.numpy as jnp
import numpy as np
from jax import lax
from jax.experimental import pallas as pl
from jax.experimental.pallas import tpu as pltpu
from jax.sharding import PartitionSpec as P

screening = 0.0428
MESH = pl.DeviceIdType.MESH
N = 128
LINES = 4
PEERS = 32
BANDS = 8
BLOCK = 8 * LINES


def complex_matrix(sign):
    points = np.arange(N)
    angle = (points[:, None] * points[None, :] % N) * (2.0 * math.pi / N)
    cosine, sine = np.cos(angle), sign * np.sin(angle)
    return np.block([[cosine, -sine], [sine, cosine]])


def peer_major():
    peer, part, line = np.meshgrid(np.arange(PEERS), np.arange(2), np.arange(LINES), indexing="ij")
    return (part * N + peer * LINES + line).reshape(-1)


def line_major():
    line, part, peer = np.meshgrid(np.arange(LINES), np.arange(2), np.arange(PEERS), indexing="ij")
    return (part * N + peer * LINES + line).reshape(-1)


def tables():
    forward, inverse = complex_matrix(-1), complex_matrix(1)
    peers, lines = peer_major(), line_major()
    return np.stack(
        [
            forward.T,
            forward[peers],
            forward[:, lines],
            inverse[lines],
            inverse[:, lines],
            inverse.T,
        ]
    ).astype(np.float32)


def split(x):
    high = x.astype(jnp.bfloat16)
    return high, (x - high.astype(jnp.float32)).astype(jnp.bfloat16)


def product(a, b):
    dot = functools.partial(jnp.dot, preferred_element_type=jnp.float32)
    return dot(a[0], b[0]) + (dot(a[0], b[1]) + dot(a[1], b[0]))


def signed(index):
    return jnp.where(index < N // 2, index, index - N).astype(jnp.float32) * (2.0 * math.pi / N)


def filter_values(me):
    shape = (N, LINES * N)
    lane = lax.broadcasted_iota(jnp.int32, shape, 1)
    kx = signed(lax.broadcasted_iota(jnp.int32, shape, 0))
    ky = signed(me * LINES + lane // N)
    kz = signed(lane % N)
    square = kx * kx + ky * ky + kz * kz
    positive = square > 0
    safe = jnp.where(positive, square, 1.0)
    value = 4.0 * math.pi * (1.0 - jnp.exp(-safe / (4.0 * screening * screening))) / safe
    value = jnp.where(positive, value, math.pi / (screening * screening))
    return value * (-0.25 / float(N * N * N))


def kernel(
    orb_hbm, table_hbm, kept_hbm, returned_hbm,
    home, own, exact, table, received, filt, out_a, in_a, out_b, in_b, back, total,
    table_sem, own_recv, received_recv, shift_send, lent_send,
    a_send, a_recv, b_send, b_recv, ret_send, ret_recv, kept_send, kept_recv,
):
    grid, band = lax.axis_index("grid"), lax.axis_index("band")
    upper, odd = lax.div(grid, PEERS // 2), lax.rem(band, 2)
    partner = band + 1 - 2 * odd
    lower = upper == 0
    lower_band = band + upper * (partner - band)
    upper_band = band + (1 - upper) * (partner - band)
    upper_even = upper * (1 - odd) == 1
    upper_odd = upper * odd == 1

    def around(by):
        return lax.rem(band + (by + BANDS) % BANDS, BANDS)

    def peer(k):
        to = grid + k
        to = jnp.where(to >= PEERS, to - PEERS, to)
        return to, {"band": jnp.where(to >= PEERS // 2, upper_band, lower_band), "grid": to}

    load_home = pltpu.make_async_copy(orb_hbm, home, table_sem.at[1])
    load_home.start()
    load_table = pltpu.make_async_copy(table_hbm, exact, table_sem.at[0])
    load_table.start()

    barrier = pltpu.get_barrier_semaphore()

    def greet_band(to):
        pl.semaphore_signal(barrier, inc=1, device_id={"band": to}, device_id_type=MESH)

    @pl.when(lower)
    def _():
        greet_band(around(1))
        greet_band(around(-1))

    @pl.when(upper == 1)
    def _():
        greet_band(partner)

    @pl.when(upper_odd)
    def _():
        greet_band(around(2))
        greet_band(around(-2))

    def greet(k, carry):
        pl.semaphore_signal(barrier, inc=1, device_id=peer(k)[1], device_id_type=MESH)
        return carry

    lax.fori_loop(1, PEERS, greet, 0)
    pl.semaphore_wait(barrier, PEERS - 1 + (1 - upper) * 2 + upper * (1 + 2 * odd))

    load_home.wait()

    def pass_on(source, target, send_sem, recv_sem, to):
        pltpu.make_async_remote_copy(
            src_ref=source, dst_ref=target, send_sem=send_sem, recv_sem=recv_sem,
            device_id={"band": to}, device_id_type=MESH,
        ).start()

    def stay(source, target, sem):
        pltpu.make_async_copy(source, target, sem).start()

    def await_copy(ref, sem):
        pltpu.make_async_copy(ref, ref, sem).wait()

    pairs = [(c, x) for x in range(LINES) for c in range(2)]
    slabs = [(j, x) for j in range(2) for x in range(LINES)]

    @pl.when(lower)
    def _():
        for j, x in slabs:
            pass_on(
                home.at[j, x], received.at[j, x], shift_send.at[0], received_recv.at[j, x], around(1)
            )
        for c, x in pairs:
            stay(home.at[c, x], own.at[c, x], own_recv.at[c, x])

    @pl.when(upper == 1)
    def _():
        for c, x in pairs:
            pass_on(home.at[c, x], own.at[c, x], shift_send.at[0], own_recv.at[c, x], partner)

    @pl.when(upper_even)
    def _():
        for j, x in slabs:
            stay(home.at[j, x], received.at[j, x], received_recv.at[j, x])

    @pl.when(upper_odd)
    def _():
        for j, x in slabs:
            pass_on(
                home.at[j, x], received.at[j, x], lent_send.at[0], received_recv.at[j, x], around(2)
            )

    def split_table(index):
        table[index, 0], table[index, 1] = split(exact[index])

    def prepare_return():
        filt[...] = filter_values(grid)
        for index in range(2, 6):
            split_table(index)

    load_table.wait()
    split_table(0)
    split_table(1)

    def exchange(source, target, send_sem, recv_sem, by_core=False):
        def send(to, device):
            pltpu.make_async_remote_copy(
                src_ref=source(to), dst_ref=target(grid),
                send_sem=send_sem, recv_sem=recv_sem,
                device_id=device, device_id_type=MESH,
            ).start()

        def next_peer(k, carry):
            send(*peer(k))
            return carry

        def next_chip(i, core):
            chip = lax.div(grid, 2) + i
            chip = jnp.where(chip >= PEERS // 2, chip - PEERS // 2, chip)
            to = chip * 2 + core

            @pl.when(to != grid)
            def _():
                group = jnp.where(chip >= PEERS // 4, upper_band, lower_band)
                send(to, {"band": group, "grid": to})

            return core

        if by_core:
            for core in range(2):
                lax.fori_loop(0, PEERS // 2, next_chip, core)
        else:
            lax.fori_loop(1, PEERS, next_peer, 0)

    def await_rows(target, rows, sem):
        some = target.at[pl.ds(0, (PEERS - 1) * rows)]
        pltpu.make_async_copy(some, some, sem).wait()

    def gather(target, units):
        return jnp.concatenate(
            [target[pl.ds(unit, PEERS, stride=BLOCK), :] for unit in units], axis=0
        )

    def weights(index):
        return table[index, 0], table[index, 1]

    def unit(x, part, line):
        return x * 8 + part * LINES + line

    def spectra(j, planes):
        partner = received[j, planes]
        count = partner.shape[0]
        field = jnp.concatenate(
            [(own[c, planes] * partner).reshape(count * N, N) for c in range(2)], axis=1
        )
        lines = product(split(field), weights(0))
        stacked = jnp.concatenate(
            [
                jnp.concatenate(
                    [lines[x * N : (x + 1) * N, c * N : (c + 1) * N] for x in range(count)], axis=1
                )
                for c in range(2)
            ],
            axis=0,
        )
        result = product(weights(1), split(stacked)).reshape(PEERS, 8, count * N)
        for i in range(count):
            x = planes.start + i
            out_a[j, :, x * 8 : (x + 1) * 8, :] = result[:, :, i * N : (i + 1) * N]

    def send_spectra(j, planes):
        rows = pl.ds(planes.start * 8, (planes.stop - planes.start) * 8)
        first = planes.start * 8
        size = (planes.stop - planes.start) * 8
        exchange(
            lambda to: out_a.at[j, to, rows],
            lambda me: in_a.at[j, pl.ds(me * BLOCK + first, size)],
            a_send.at[j], a_recv.at[j],
        )

    def keep(j, target, block):
        target[j, pl.ds(pl.multiple_of(grid * BLOCK, BLOCK), BLOCK), :] = block

    for x in range(LINES):
        for c in range(2):
            await_copy(own.at[c, x], own_recv.at[c, x])
        await_copy(received.at[0, x], received_recv.at[0, x])
        spectra(0, slice(x, x + 1))
        send_spectra(0, slice(x, x + 1))
    keep(0, in_a, out_a[0, grid])
    for x in range(LINES):
        await_copy(received.at[1, x], received_recv.at[1, x])
    spectra(1, slice(0, LINES))
    send_spectra(1, slice(0, LINES))
    keep(1, in_a, out_a[1, grid])
    prepare_return()

    def filtered(j):
        gathered = jnp.concatenate(
            [
                gather(
                    in_a.at[j],
                    [unit(x, part, line) for x in range(LINES) for part in range(2)],
                )
                for line in range(LINES)
            ],
            axis=1,
        )
        spectrum = product(weights(2), split(gathered))
        values = filt[...]
        spectrum = jnp.concatenate([spectrum[:N] * values, spectrum[N:] * values], axis=0)
        result = product(weights(3), split(spectrum))
        target = out_b.at[j]
        for x in range(LINES):
            for part in range(2):
                first = (x * 2 + part) * PEERS
                for line in range(LINES):
                    target[pl.ds(unit(x, part, line), PEERS, stride=BLOCK), :] = result[
                        first : first + PEERS, line * N : (line + 1) * N
                    ]

    def send_filtered(j, x, count, sem):
        size = count * 8
        exchange(
            lambda to: out_b.at[j, pl.ds(to * BLOCK + x * 8, size)],
            lambda me: in_b.at[j, pl.ds(me * BLOCK + x * 8, size)],
            b_send.at[sem], b_recv.at[sem], sem > 0,
        )

    for j in range(2):
        await_rows(in_a.at[j], BLOCK, a_recv.at[j])
        filtered(j)
        if j == 0:
            send_filtered(j, 0, LINES, 0)
        else:
            for x in range(LINES):
                send_filtered(j, x, 1, 1 + x)
        keep(j, in_b, out_b[j, pl.ds(pl.multiple_of(grid * BLOCK, BLOCK), BLOCK), :])

    def finish(j, x):
        gathered = gather(
            in_b.at[j],
            [unit(x, part, line) for line in range(LINES) for part in range(2)],
        )
        plane = product(weights(4), split(gathered))
        plane = jnp.concatenate([plane[:N], plane[N:]], axis=1)
        potential = product(split(plane), weights(5))
        parts = [potential[:, c * N : (c + 1) * N] for c in range(2)]
        back[j, x] = parts[0] * own[0, x] + parts[1] * own[1, x]
        for c in range(2):
            term = parts[c] * received[j, x]
            total[c, x] = term if j == 0 else total[c, x] + term

        @pl.when(lower)
        def _():
            pass_on(back.at[j, x], returned_hbm.at[j, x], ret_send.at[0], ret_recv.at[0], around(-1))
            if j == 1:
                for c in range(2):
                    stay(total.at[c, x], kept_hbm.at[c, x], kept_recv.at[0])

        if j == 1:

            @pl.when(upper == 1)
            def _():
                for c in range(2):
                    pass_on(
                        total.at[c, x], returned_hbm.at[c, x], ret_send.at[0], ret_recv.at[0], partner
                    )

        @pl.when(upper_even)
        def _():
            stay(back.at[j, x], kept_hbm.at[j, x], kept_recv.at[0])

        @pl.when(upper_odd)
        def _():
            pass_on(back.at[j, x], kept_hbm.at[j, x], kept_send.at[0], kept_recv.at[0], around(-2))

    await_rows(in_b.at[0], BLOCK, b_recv.at[0])
    for x in range(LINES):
        finish(0, x)
    for x in range(LINES):
        await_rows(in_b.at[1], 8, b_recv.at[1 + x])
        finish(1, x)

    await_copy(own, shift_send.at[0])
    for j in range(2):
        await_rows(in_a.at[j], BLOCK, a_send.at[j])
    await_rows(in_b.at[0], BLOCK, b_send.at[0])
    for x in range(LINES):
        await_rows(in_b.at[1], 8, b_send.at[1 + x])

    @pl.when(upper_odd)
    def _():
        await_copy(own, lent_send.at[0])
        await_copy(back, kept_send.at[0])

    await_copy(back, ret_send.at[0])
    await_copy(kept_hbm, kept_recv.at[0])
    await_copy(returned_hbm, ret_recv.at[0])


def per_device(orbitals, table):
    slab = (2, LINES, N, N)
    block = (2, PEERS, BLOCK, N)
    flat = (2, PEERS * BLOCK, N)
    f32 = jnp.float32
    dma = pltpu.SemaphoreType.DMA
    kept, returned = pl.pallas_call(
        kernel,
        out_shape=[jax.ShapeDtypeStruct(slab, f32)] * 2,
        in_specs=[pl.BlockSpec(memory_space=pltpu.HBM)] * 2,
        out_specs=[pl.BlockSpec(memory_space=pltpu.HBM)] * 2,
        scratch_shapes=[
            pltpu.VMEM(slab, f32),
            pltpu.VMEM(slab, f32),
            pltpu.VMEM(table.shape, f32),
            pltpu.VMEM((table.shape[0], 2, 2 * N, 2 * N), jnp.bfloat16),
            pltpu.VMEM(slab, f32),
            pltpu.VMEM((N, LINES * N), f32),
            pltpu.VMEM(block, f32),
            pltpu.VMEM(flat, f32),
            pltpu.VMEM(flat, f32),
            pltpu.VMEM(flat, f32),
            pltpu.VMEM(slab, f32),
            pltpu.VMEM(slab, f32),
            dma((2,)),
            dma((2, LINES)),
            dma((2, LINES)),
            dma((1,)),
            dma((1,)),
            dma((2,)),
            dma((2,)),
            dma((1 + LINES,)),
            dma((1 + LINES,)),
            dma((1,)),
            dma((1,)),
            dma((1,)),
            dma((1,)),
        ],
        compiler_params=pltpu.CompilerParams(
            collective_id=0, has_side_effects=True, vmem_limit_bytes=int(52.65 * 2**20)
        ),
    )(orbitals, table)
    return kept + returned


def solution(mesh):
    body = jax.shard_map(
        per_device,
        mesh=mesh,
        in_specs=(P("band", "grid", None, None), P()),
        out_specs=P("band", "grid", None, None),
        check_vma=False,
    )
    constants = tables()
    return lambda orbitals: body(orbitals, jnp.asarray(constants))
```

profile of v0, /device:TPU:1, one launch (start us, length us, event | category | flops | bytes accessed | tf_op | source)
XLA Modules:
  0.0 68.1 jit_solution(11227096569695576165)
XLA Ops:
  0.0 67.2 %shard_map.28 = (f32[2,4,128,128]{3,2,1,0:T(8,128)S(1)}, f32[2,4,128,128]{3,2,1,0:T(8,128)S(1)}) custom-call(f32[2,4,128,128]{3,2,1,0:T(8,128)} %orb_hbm.1, f32[6,256,256]{2,1,0:T(8,128)} %constant.2.clone.table_hbm), custom_call_target="tpu_custom_call" | custom-call | tf_op jit(solution)/shard_map/pallas_call | solution.py:393
  67.2 0.9 %add.3 = f32[2,4,128,128]{3,2,1,0:T(8,128)} add(f32[2,4,128,128]{3,2,1,0:T(8,128)S(1)} %get-tuple-element.7, f32[2,4,128,128]{3,2,1,0:T(8,128)S(1)} %get-tuple-element.8) | non-fusion elementwise | flops 131072 | bytes 1572864 | tf_op jit(solution)/shard_map/add | solution.py:429
where the time goes:
time: 68.2 us; the launch traced here: 68.1 us
  Pallas kernels  67.2 us (99%)
  other arithmetic  0.85 us (1%)
    pallas_call x1, Pallas kernels, per_device(): pl.pallas_call(kernel, out_shape=[jax.ShapeDtypeStruct(slab, f32)] * 2, i...  67.2 us

commit v1 on v0

--- a/solution.py
+++ b/solution.py
@@ -309,7 +309,7 @@
         exchange(
             lambda to: out_b.at[j, pl.ds(to * BLOCK + x * 8, size)],
             lambda me: in_b.at[j, pl.ds(me * BLOCK + x * 8, size)],
-            b_send.at[sem], b_recv.at[sem], sem > 0,
+            b_send.at[sem], b_recv.at[sem], True,
         )
 
     for j in range(2):
@@ -331,10 +331,20 @@
         plane = jnp.concatenate([plane[:N], plane[N:]], axis=1)
         potential = product(split(plane), weights(5))
         parts = [potential[:, c * N : (c + 1) * N] for c in range(2)]
-        back[j, x] = parts[0] * own[0, x] + parts[1] * own[1, x]
         for c in range(2):
             term = parts[c] * received[j, x]
             total[c, x] = term if j == 0 else total[c, x] + term
+
+        if j == 1:
+
+            @pl.when(upper == 1)
+            def _():
+                for c in range(2):
+                    pass_on(
+                        total.at[c, x], returned_hbm.at[c, x], ret_send.at[0], ret_recv.at[0], partner
+                    )
+
+        back[j, x] = parts[0] * own[0, x] + parts[1] * own[1, x]
 
         @pl.when(lower)
         def _():
@@ -342,15 +352,6 @@
             if j == 1:
                 for c in range(2):
                     stay(total.at[c, x], kept_hbm.at[c, x], kept_recv.at[0])
-
-        if j == 1:
-
-            @pl.when(upper == 1)
-            def _():
-                for c in range(2):
-                    pass_on(
-                        total.at[c, x], returned_hbm.at[c, x], ret_send.at[0], ret_recv.at[0], partner
-                    )
 
         @pl.when(upper_even)
         def _():

time: 68.2 us -> 68.1 us (level)
  no operation moved by 1% of the time
where the time goes in v1:
time: 68.1 us; the launch traced here: 68 us
  Pallas kernels  67.2 us (99%)
  other arithmetic  0.85 us (1%)
    pallas_call x1, Pallas kernels, per_device(): pl.pallas_call(kernel, out_shape=[jax.ShapeDtypeStruct(slab, f32)] * 2, i...  67.2 us

profile of v1, /device:TPU:1, one launch (start us, length us, event | category | flops | bytes accessed | tf_op | source)
XLA Modules:
  0.0 68.0 jit_solution(7001157455983977224)
XLA Ops:
  0.0 67.2 %shard_map.28 = (f32[2,4,128,128]{3,2,1,0:T(8,128)S(1)}, f32[2,4,128,128]{3,2,1,0:T(8,128)S(1)}) custom-call(f32[2,4,128,128]{3,2,1,0:T(8,128)} %orb_hbm.1, f32[6,256,256]{2,1,0:T(8,128)} %constant.2.clone.table_hbm), custom_call_target="tpu_custom_call" | custom-call | tf_op jit(solution)/shard_map/pallas_call | solution.py:394
  67.2 0.9 %add.3 = f32[2,4,128,128]{3,2,1,0:T(8,128)} add(f32[2,4,128,128]{3,2,1,0:T(8,128)S(1)} %get-tuple-element.7, f32[2,4,128,128]{3,2,1,0:T(8,128)S(1)} %get-tuple-element.8) | non-fusion elementwise | flops 131072 | bytes 1572864 | tf_op jit(solution)/shard_map/add | solution.py:430

commit v2 on v1

--- a/solution.py
+++ b/solution.py
@@ -309,7 +309,7 @@
         exchange(
             lambda to: out_b.at[j, pl.ds(to * BLOCK + x * 8, size)],
             lambda me: in_b.at[j, pl.ds(me * BLOCK + x * 8, size)],
-            b_send.at[sem], b_recv.at[sem], True,
+            b_send.at[sem], b_recv.at[sem], sem > 0,
         )
 
     for j in range(2):

time: 68.1 us -> 68.2 us (level)
  no operation moved by 1% of the time
where the time goes in v2:
time: 68.2 us; the launch traced here: 68.1 us
  Pallas kernels  67.2 us (99%)
  other arithmetic  0.85 us (1%)
    pallas_call x1, Pallas kernels, per_device(): pl.pallas_call(kernel, out_shape=[jax.ShapeDtypeStruct(slab, f32)] * 2, i...  67.2 us

profile of v2, /device:TPU:1, one launch (start us, length us, event | category | flops | bytes accessed | tf_op | source)
XLA Modules:
  0.0 68.1 jit_solution(9229067828530536134)
XLA Ops:
  0.0 67.2 %shard_map.28 = (f32[2,4,128,128]{3,2,1,0:T(8,128)S(1)}, f32[2,4,128,128]{3,2,1,0:T(8,128)S(1)}) custom-call(f32[2,4,128,128]{3,2,1,0:T(8,128)} %orb_hbm.1, f32[6,256,256]{2,1,0:T(8,128)} %constant.2.clone.table_hbm), custom_call_target="tpu_custom_call" | custom-call | tf_op jit(solution)/shard_map/pallas_call | solution.py:394
  67.2 0.9 %add.3 = f32[2,4,128,128]{3,2,1,0:T(8,128)} add(f32[2,4,128,128]{3,2,1,0:T(8,128)S(1)} %get-tuple-element.7, f32[2,4,128,128]{3,2,1,0:T(8,128)S(1)} %get-tuple-element.8) | non-fusion elementwise | flops 131072 | bytes 1572864 | tf_op jit(solution)/shard_map/add | solution.py:430
